TPU v7x, 512 devices: a whole 4x8x8 slice. The times are simulated.
512 devices in a mesh: chan: 8 (over y_lo, core), seg: 64 (over y_hi, z, x).
Axes of the slice: x: 4, y: 8 (y_hi: 2, y_lo: 4; y = y_hi * 4 + y_lo), z: 8, core: 2. Of those that a mesh axis runs over, the one named last changes fastest.
Arguments:
- waveforms: bfloat16 [512, 512, 1536], P('seg', 'chan'), may hold values from -6 to 6
- segment_keep: int32 [512], P('seg'), may hold values 0 or 1
- channel_good: int32 [512], P('chan'), may hold values 0 or 1
Outputs:
- correlations: bfloat16 [512, 512, 2560], P('chan', 'seg')
Inputs may be any that keep to these rules, and one draw needn't show every extreme that they name: `segment_keep`: 1 keeps the segment, 0 drops it. `channel_good`: 1 marks a working channel, 0 a dead one.
All inputs are finite; a program needn't handle non-finite values. No bound on the sum of `segment_keep` or of `channel_good` on one device may be relied on, other than what follows from the above.
Results may differ from a plain program's by a relative error of at most 0.0076.
Values may be sent and summed in bfloat16 or wider, within the bound.
A program may use at most 64 MiB of HBM per device.

v0:
```python
import functools

import jax
import jax.numpy as jnp
import ml_dtypes
import numpy as np
from jax import lax
from jax.experimental import pallas as pl
from jax.experimental.pallas import tpu as pltpu
from jax.sharding import PartitionSpec as P

NT = 1536
BINS = 384
LOWEST = 12
LAGS = 2560
SEGS = 512
MESH = pl.DeviceIdType.MESH
F32 = jnp.float32
BF16 = jnp.bfloat16


def forward_rows():
    t = np.arange(NT, dtype=np.int64)
    f = LOWEST + np.arange(BINS, dtype=np.int64)
    theta = np.float32(2.0 * np.pi / (2 * NT)) * ((f[:, None] * t[None, :]) % (2 * NT)).astype(np.float32)
    theta = theta.astype(np.float64)
    rows = np.concatenate([np.cos(theta), -np.sin(theta)], axis=0) / np.sqrt(NT)
    return rows.astype(np.float32).astype(ml_dtypes.bfloat16)


def lag_rows():
    f = LOWEST + np.arange(BINS, dtype=np.int64)
    l = np.arange(LAGS, dtype=np.int64) - LAGS // 2
    phi = np.float32(2.0 * np.pi / (2 * NT)) * ((f[:, None] * l[None, :]) % (2 * NT)).astype(np.float32)
    phi = phi.astype(np.float64)
    rows = np.concatenate([np.cos(phi), -np.sin(phi)], axis=0)
    return rows.astype(np.float32).astype(ml_dtypes.bfloat16)


def device_of(row, column):
    y, core = row // 2, row % 2
    return ((y % 4) * 2 + core, (y // 4) * 32 + column)


def share(row, column):
    return (row // 2 + 2 * (row % 2) + column // 4 + column % 4) % 4


def column_slot(row, column):
    return (row % 2) * 6 + (row // 8) * 3 + share(row, column) - 1


def row_slot(row, column):
    return (column // 4) * 3 + share(row, column) - 1


def bin_place(f, core):
    in_0 = f < 192
    y0, slot24 = f // 24, f % 24
    z0, r0 = slot24 // 3, slot24 % 3
    x0 = (r0 + 1 - y0 - z0 + 32) % 4
    g = f - 192
    g = jnp.where(in_0, 0, g)
    c1, slot6 = g // 6, g % 6
    yh1, r1 = slot6 // 3, slot6 % 3
    yl1 = (r1 + 1 - 2 - c1 // 4 - c1 % 4 + 32) % 4
    place_0 = jnp.where(in_0, (z0 * 4 + x0) * 12 + (y0 // 4) * 3 + r0, c1 * 12 + 6 + slot6)
    place_1 = jnp.where(in_0, (y0 * 2) * 24 + slot24, ((yh1 * 4 + yl1) * 2 + 1) * 24 + (c1 // 4) * 3 + r1)
    return jnp.where(core == 0, place_0, place_1)


def stack_kernel(
    wave, table, keep, good, lhs_out,
    spec, mag, sent, mid_a, mid_b, got, gram_in, cross, back_a, back_b, done_a, done_b, rows_f, lhs_f,
    send_sem, recv_sem, local_sem,
):
    chan = lax.axis_index("chan")
    seg = lax.axis_index("seg")
    core = chan % 2
    y = (seg // 32) * 4 + chan // 2
    column = seg % 32
    z, x = column // 4, column % 4
    row = y * 2 + core
    y8 = (chan // 2) * 2 + seg // 32
    owner = share(row, column) != 0

    def next_column(k):
        return ((z + k // 4) % 8) * 4 + (x + k) % 4

    def next_row(k):
        return ((y + k // 2) % 8) * 2 + (core + k) % 2

    barrier = pltpu.get_barrier_semaphore()

    @pl.loop(1, 32)
    def _(k):
        pl.semaphore_signal(barrier, inc=1, device_id=device_of(row, next_column(k)), device_id_type=MESH)

    @pl.loop(1, 16)
    def _(k):
        pl.semaphore_signal(barrier, inc=1, device_id=device_of(next_row(k), column), device_id_type=MESH)

    def remote(src, dst, n, to_row, to_column):
        return pltpu.make_async_remote_copy(
            src_ref=src, dst_ref=dst, send_sem=send_sem.at[n], recv_sem=recv_sem.at[n],
            device_id=device_of(to_row, to_column), device_id_type=MESH,
        )

    def local(src, dst, n):
        return pltpu.make_async_copy(src, dst, local_sem.at[n])

    def wait_bytes(ref, sem):
        pltpu.make_async_copy(ref, ref, sem).wait()

    @pl.loop(0, 2)
    def _(half):
        cols = pl.ds(pl.multiple_of(half * 256, 256), 256)
        spec[:, cols] = lax.dot_general(
            table[...], wave[cols, :], (((1,), (1,)), ((), ())), preferred_element_type=F32
        )

    def add_magnitude(g, total):
        at = pl.multiple_of(g * 8, 8)
        re = spec[pl.ds(at, 8), :]
        im = spec[pl.ds(pl.multiple_of(BINS + at, 8), 8), :]
        m = jnp.sqrt(re * re + im * im)
        mag[pl.ds(at, 8), :] = m
        return total + m

    total = lax.fori_loop(0, BINS // 8, add_magnitude, jnp.zeros((8, 512), F32), unroll=4)
    water = 0.5 * (jnp.sum(total, axis=0, keepdims=True) * (1.0 / BINS)) + 1e-06
    good_f = good[...].astype(F32)
    good_2 = jnp.concatenate([good_f, good_f], axis=1)
    lane = lax.broadcasted_iota(jnp.int32, (1, 128), 1)
    lower = lane < 64
    flags = jnp.concatenate(
        [good_2 * jnp.where(lower, keep[2 * t].astype(F32), keep[2 * t + 1].astype(F32)) for t in range(4)], axis=1
    )
    lower8 = lax.broadcasted_iota(jnp.int32, (8, 128), 1) < 64

    @pl.loop(0, BINS // 8)
    def _(g):
        at = pl.multiple_of(g * 8, 8)
        weight = flags / jnp.maximum(mag[pl.ds(at, 8), :], water)
        re = spec[pl.ds(at, 8), :] * weight
        im = spec[pl.ds(pl.multiple_of(BINS + at, 8), 8), :] * weight
        by_s = []
        for t in range(4):
            r_t, i_t = re[:, 128 * t : 128 * t + 128], im[:, 128 * t : 128 * t + 128]
            by_s.append(jnp.where(lower8, r_t, pltpu.roll(i_t, 64, 1)))
            by_s.append(jnp.where(lower8, pltpu.roll(r_t, 64, 1), i_t))
        units = jnp.swapaxes(jnp.stack(by_s, axis=0), 0, 1)
        for k in range(8):
            sent[bin_place(g * 8 + k, core)] = units[k].astype(BF16)

    pl.semaphore_wait(barrier, 46)

    @pl.when(core == 0)
    def _():
        local(sent.at[pl.ds(column * 12, 12)], mid_a.at[column], 0).start()

        @pl.loop(1, 32)
        def _(k):
            to = next_column(k)
            remote(sent.at[pl.ds(to * 12, 12)], mid_a.at[column], 0, row, to).start()

    @pl.when(core == 1)
    def _():
        local(sent.at[pl.ds(row * 24, 24)], mid_b.at[y8], 1).start()

        @pl.loop(1, 16)
        def _(k):
            to = next_row(k)
            remote(sent.at[pl.ds(to * 24, 24)], mid_b.at[y8], 1, to, column).start()

    @pl.when(core == 0)
    def _():
        wait_bytes(mid_a.at[pl.ds(0, 31)], recv_sem.at[0])
        wait_bytes(mid_a.at[0], local_sem.at[0])

        @pl.loop(1, 16)
        def _(k):
            to = next_row(k)

            @pl.when(share(to, column) != 0)
            def _():
                remote(mid_a.at[:, column_slot(to, column)], got.at[0, y8], 2, to, column).start()

        @pl.when(owner)
        def _():
            local(mid_a.at[:, column_slot(row, column)], got.at[0, y8], 2).start()

        wait_bytes(mid_b, recv_sem.at[1])

    @pl.when(core == 1)
    def _():
        wait_bytes(mid_b.at[pl.ds(0, 7)], recv_sem.at[1])
        wait_bytes(mid_b.at[0], local_sem.at[1])

    @pl.loop(1, 32)
    def _(k):
        to = next_column(k)

        @pl.when(share(row, to) != 0)
        def _():
            remote(mid_b.at[:, row_slot(row, to)], got.at[1, :, column], 3, row, to).start()

    @pl.when(owner)
    def _():
        local(mid_b.at[:, row_slot(row, column)], got.at[1, :, column], 3).start()
        wait_bytes(got.at[1, :, 0], local_sem.at[3])
        wait_bytes(got.at[1, :, pl.ds(0, 31)], recv_sem.at[3])

        @pl.when(core == 0)
        def _():
            wait_bytes(got.at[0, 0], local_sem.at[2])
            wait_bytes(got.at[0, pl.ds(0, 7)], recv_sem.at[2])

        @pl.when(core == 1)
        def _():
            wait_bytes(got.at[0], recv_sem.at[2])

        for c in range(2):
            for yl in range(4):
                block = got[c, 2 * yl : 2 * yl + 2].astype(F32).reshape(512, 128).astype(BF16)
                gram_in[:, 128 * (4 * c + yl) : 128 * (4 * c + yl) + 128] = block
        sign = jnp.where(lower, 1.0, -1.0).astype(F32)
        b_ids = lax.broadcasted_iota(jnp.int32, (64, 128), 0)
        a_ids = lax.broadcasted_iota(jnp.int32, (64, 128), 1) % 64

        @pl.loop(0, 4)
        def _(pair):
            products = lax.dot_general(
                gram_in[:, pl.ds(pl.multiple_of(pair * 256, 256), 256)], gram_in[...],
                (((0,), (0,)), ((), ())), preferred_element_type=F32,
            )
            for second in range(2):
                i = pair * 2 + second
                chan_b = (i % 4) * 2 + i // 4
                for j in range(8):
                    chan_a = (j % 4) * 2 + j // 4
                    tile = products[128 * second : 128 * second + 128, 128 * j : 128 * j + 128]
                    summed = tile[:64] + sign * pltpu.roll(tile[64:], 64, 1)
                    summed = jnp.where(jnp.logical_and(b_ids == a_ids, i == j), 0.0, summed)
                    for part in range(8):
                        seg_b = chan_b * 8 + part
                        to_row = ((seg_b // 32) * 4 + chan_a // 2) * 2 + chan_a % 2
                        to_column = seg_b % 32
                        place = jnp.where(core == 0, to_column * 16 + to_row, to_row * 32 + to_column)
                        cross[place] = summed[8 * part : 8 * part + 8].astype(BF16)

        @pl.when(core == 0)
        def _():
            slot = row_slot(row, column)
            local(cross.at[pl.ds(column * 16, 16)], back_a.at[slot], 4).start()

            @pl.loop(1, 32)
            def _(k):
                to = next_column(k)
                remote(cross.at[pl.ds(to * 16, 16)], back_a.at[slot], 4, row, to).start()

        @pl.when(core == 1)
        def _():
            slot = column_slot(row, column) - 6
            local(cross.at[pl.ds(row * 32, 32)], back_b.at[slot], 5).start()

            @pl.loop(1, 16)
            def _(k):
                to = next_row(k)
                remote(cross.at[pl.ds(to * 32, 32)], back_b.at[slot], 5, to, column).start()

    @pl.when(core == 0)
    def _():
        @pl.when(owner)
        def _():
            wait_bytes(back_a.at[0], local_sem.at[4])
            wait_bytes(back_a.at[pl.ds(0, 23)], recv_sem.at[4])

        @pl.when(jnp.logical_not(owner))
        def _():
            wait_bytes(back_a, recv_sem.at[4])

        @pl.loop(1, 16)
        def _(k):
            to = next_row(k)
            remote(back_a.at[:, to], done_a.at[y], 6, to, column).start()

        local(back_a.at[:, row], done_a.at[y], 6).start()

    own_back = jnp.logical_and(owner, core == 1)

    @pl.when(own_back)
    def _():
        wait_bytes(back_b.at[0], local_sem.at[5])
        wait_bytes(back_b.at[pl.ds(0, 5)], recv_sem.at[5])

    @pl.when(jnp.logical_not(own_back))
    def _():
        wait_bytes(back_b, recv_sem.at[5])

    @pl.loop(1, 32)
    def _(k):
        to = next_column(k)
        remote(back_b.at[:, to], done_b.at[column], 7, row, to).start()

    local(back_b.at[:, column], done_b.at[column], 7).start()

    @pl.when(core == 0)
    def _():
        wait_bytes(done_a.at[0], local_sem.at[6])
        wait_bytes(done_a.at[pl.ds(0, 7)], recv_sem.at[6])

    @pl.when(core == 1)
    def _():
        wait_bytes(done_a, recv_sem.at[6])

    wait_bytes(done_b.at[0], local_sem.at[7])
    wait_bytes(done_b.at[pl.ds(0, 31)], recv_sem.at[7])

    rows_f[0:1536] = done_a[...].astype(F32).reshape(1536, 128)
    rows_f[1536:3072] = done_b[...].astype(F32).reshape(1536, 128)
    for b in range(8):
        turned = rows_f[pl.ds(b, BINS, stride=8), :].T
        for p in range(2):
            for k in range(3):
                lhs_f[3 * p + k, pl.ds(b, 64, stride=8), :] = turned[64 * p : 64 * p + 64, 128 * k : 128 * k + 128]
    for k in range(6):
        lhs_out[:, 128 * k : 128 * k + 128] = lhs_f[k].astype(BF16)

    @pl.when(core == 0)
    def _():
        wait_bytes(mid_a.at[pl.ds(0, 31)], send_sem.at[0])

        @pl.when(owner)
        def _():
            wait_bytes(got.at[0, pl.ds(0, 8)], send_sem.at[2])
            wait_bytes(got.at[0, pl.ds(0, 3)], send_sem.at[2])
            wait_bytes(cross.at[pl.ds(0, 31 * 16)], send_sem.at[4])

        @pl.when(jnp.logical_not(owner))
        def _():
            wait_bytes(got.at[0, pl.ds(0, 8)], send_sem.at[2])
            wait_bytes(got.at[0, pl.ds(0, 4)], send_sem.at[2])

        wait_bytes(done_a.at[pl.ds(0, 8)], send_sem.at[6])
        wait_bytes(done_a.at[pl.ds(0, 7)], send_sem.at[6])

    @pl.when(core == 1)
    def _():
        wait_bytes(sent.at[pl.ds(0, 15 * 24)], send_sem.at[1])

        @pl.when(owner)
        def _():
            wait_bytes(cross.at[pl.ds(0, 15 * 32)], send_sem.at[5])

    @pl.when(owner)
    def _():
        wait_bytes(got.at[1, :, pl.ds(0, 23)], send_sem.at[3])

    @pl.when(jnp.logical_not(owner))
    def _():
        wait_bytes(got.at[1, :, pl.ds(0, 24)], send_sem.at[3])

    wait_bytes(done_b.at[pl.ds(0, 31)], send_sem.at[7])


def stacked(wave, table, keep, good):
    vmem = pl.BlockSpec(memory_space=pltpu.VMEM)
    return pl.pallas_call(
        stack_kernel,
        out_shape=jax.ShapeDtypeStruct((512, 2 * BINS), BF16),
        in_specs=[vmem, vmem, pl.BlockSpec(memory_space=pltpu.SMEM), vmem],
        out_specs=vmem,
        scratch_shapes=[
            pltpu.VMEM((2 * BINS, 512), F32),
            pltpu.VMEM((BINS, 512), F32),
            pltpu.VMEM((BINS, 8, 128), BF16),
            pltpu.VMEM((32, 12, 8, 128), BF16),
            pltpu.VMEM((8, 24, 8, 128), BF16),
            pltpu.VMEM((2, 8, 32, 8, 128), BF16),
            pltpu.VMEM((512, 1024), BF16),
            pltpu.VMEM((512, 8, 128), BF16),
            pltpu.VMEM((24, 16, 8, 128), BF16),
            pltpu.VMEM((6, 32, 8, 128), BF16),
            pltpu.VMEM((8, 24, 8, 128), BF16),
            pltpu.VMEM((32, 6, 8, 128), BF16),
            pltpu.VMEM((3072, 128), F32),
            pltpu.VMEM((6, 512, 128), F32),
            pltpu.SemaphoreType.DMA((8,)),
            pltpu.SemaphoreType.DMA((8,)),
            pltpu.SemaphoreType.DMA((8,)),
        ],
        compiler_params=pltpu.CompilerParams(collective_id=0, has_side_effects=True, vmem_limit_bytes=48 << 20),
        name="stack_cross_spectra",
    )(wave, table, keep, good)


def lag_kernel(scale, lhs, table, out):
    values = jnp.dot(lhs[...], table[...], preferred_element_type=F32) * scale
    out[...] = values.reshape(64, 8, values.shape[1]).astype(BF16)


def lagged(lhs, table, scale):
    width = 512
    return pl.pallas_call(
        functools.partial(lag_kernel, scale),
        grid=(LAGS // width,),
        out_shape=jax.ShapeDtypeStruct((64, 8, LAGS), BF16),
        in_specs=[
            pl.BlockSpec((512, 2 * BINS), lambda i: (0, 0)),
            pl.BlockSpec((2 * BINS, width), lambda i: (0, i)),
        ],
        out_specs=pl.BlockSpec((64, 8, width), lambda i: (0, 0, i)),
        compiler_params=pltpu.CompilerParams(vmem_limit_bytes=48 << 20),
        name="lag_transform",
    )(lhs, table)


def local(waveforms, segment_keep, channel_good):
    wave = waveforms.reshape(512, NT)
    lhs = stacked(wave, jnp.asarray(forward_rows()), segment_keep, channel_good.reshape(1, 64))
    return lagged(lhs, jnp.asarray(lag_rows()), float(1.0 / np.sqrt(SEGS * BINS)))


def solution(mesh):
    placed = (P("seg", "chan", None), P("seg"), P("chan"))
    return jax.shard_map(
        local, mesh=mesh, in_specs=placed, out_specs=P("chan", "seg", None), check_vma=False
    )
```

profile of v0, /device:TPU:1, one launch (start us, length us, event | category | flops | bytes accessed | tf_op | source)
XLA Modules:
  0.0 101.1 jit_solution(8515198436315224937)
XLA Ops:
  0.0 0.0 copy-start
  0.0 0.0 copy-start.1
  0.0 1.8 %copy-done.1 = bf16[768,1536]{1,0:T(8,128)(2,1)S(1)} copy-done((bf16[768,1536]{1,0:T(8,128)(2,1)S(1)}, bf16[768,1536]{1,0:T(8,128)(2,1)}, u32[]{:S(2)}) %copy-start.1) | copy-done | bytes 2359320
  1.8 0.0 copy-start.2
  1.8 1.5 %copy-done.2 = bf16[8,64,1536]{2,1,0:T(8,128)(2,1)S(1)} copy-done((bf16[8,64,1536]{2,1,0:T(8,128)(2,1)S(1)}, bf16[8,64,1536]{2,1,0:T(8,128)(2,1)}, u32[]{:S(2)}) %copy-start.2) | copy-done | bytes 1572888
  3.3 0.0 copy-start.3
  3.3 0.7 copy-done.3
  4.0 0.0 copy-start.4
  4.0 0.7 copy-done.4
  4.6 92.2 %stack_cross_spectra.1.lhs = bf16[512,768]{1,0:T(8,128)(2,1)S(1)} custom-call(bf16[512,1536]{1,0:T(8,128)(2,1)S(1)} %bitcast.2, bf16[768,1536]{1,0:T(8,128)(2,1)S(1)} %copy-done.1, s32[8]{0:T(128)S(1)} %copy-done.3, s32[1,64]{1,0:T(1,128)S(1)} %bitcast.3), custom_call_target="tpu_custom_call" | custom-call | tf_op jit(solution)/shard_map/stack_cross_spectra/pallas_call | solution.py:369
  96.8 0.0 copy-done
  96.8 4.3 %lag_transform.1 = bf16[64,8,2560]{2,1,0:T(8,128)(2,1)} custom-call(bf16[512,768]{1,0:T(8,128)(2,1)S(1)} %stack_cross_spectra.1.lhs, bf16[768,2560]{1,0:T(8,128)(2,1)S(1)} %copy-done), custom_call_target="tpu_custom_call" | custom-call | tf_op jit(solution)/shard_map/lag_transform/pallas_call | solution.py:405
Async XLA Ops:
  0.0 96.8 %copy-start = (bf16[768,2560]{1,0:T(8,128)(2,1)S(1)}, bf16[768,2560]{1,0:T(8,128)(2,1)}, u32[]{:S(2)}) copy-start(bf16[768,2560]{1,0:T(8,128)(2,1)} %constant.5.clone.table) | copy-start | bytes 11796484
  0.0 1.8 %copy-start.1 = (bf16[768,1536]{1,0:T(8,128)(2,1)S(1)}, bf16[768,1536]{1,0:T(8,128)(2,1)}, u32[]{:S(2)}) copy-start(bf16[768,1536]{1,0:T(8,128)(2,1)} %constant.4.clone.table) | copy-start | bytes 7077892
  1.8 1.5 %copy-start.2 = (bf16[8,64,1536]{2,1,0:T(8,128)(2,1)S(1)}, bf16[8,64,1536]{2,1,0:T(8,128)(2,1)}, u32[]{:S(2)}) copy-start(bf16[8,64,1536]{2,1,0:T(8,128)(2,1)} %param.5) | copy-start | bytes 4718596
  3.3 0.7 copy-start.3
  4.0 0.7 copy-start.4
where the time goes:
time: 101 us
  Pallas kernels  96.5 us (96%)
  local copies, waits for them, and re-layouts  4.61 us (5%)
    pallas_call x1, Pallas kernels, stacked(): pl.pallas_call(stack_kernel, out_shape=jax.ShapeDtypeStruct((512, 2 * BIN...  92.2 us
    unnamed x10, local copies, waits for them, and re-layouts  4.61 us
    pallas_call x1, Pallas kernels, lagged(): pl.pallas_call(functools.partial(lag_kernel, scale), grid=(LAGS // width,...  4.29 us

commit v1 on v0

v1 whole, which is shorter than its diff:
```python
import functools

import jax
import jax.numpy as jnp
import ml_dtypes
import numpy as np
from jax import lax
from jax.experimental import pallas as pl
from jax.experimental.pallas import tpu as pltpu
from jax.sharding import PartitionSpec as P

NT = 1536
BINS = 384
LOWEST = 12
LAGS = 2560
SEGS = 512
MESH = pl.DeviceIdType.MESH
F32 = jnp.float32
BF16 = jnp.bfloat16


def forward_rows():
    t = np.arange(NT, dtype=np.int64)
    f = LOWEST + np.arange(BINS, dtype=np.int64)
    theta = np.float32(2.0 * np.pi / (2 * NT)) * ((f[:, None] * t[None, :]) % (2 * NT)).astype(np.float32)
    theta = theta.astype(np.float64)
    rows = np.concatenate([np.cos(theta), -np.sin(theta)], axis=0) / np.sqrt(NT)
    return rows.astype(np.float32).astype(ml_dtypes.bfloat16)


def lag_rows():
    f = LOWEST + np.arange(BINS, dtype=np.int64)
    l = np.arange(LAGS, dtype=np.int64) - LAGS // 2
    phi = np.float32(2.0 * np.pi / (2 * NT)) * ((f[:, None] * l[None, :]) % (2 * NT)).astype(np.float32)
    phi = phi.astype(np.float64)
    rows = np.concatenate([np.cos(phi), -np.sin(phi)], axis=0)
    return rows.astype(np.float32).astype(ml_dtypes.bfloat16)


def device_of(row, column):
    y, core = row // 2, row % 2
    return ((y % 4) * 2 + core, (y // 4) * 32 + column)


def share(row, column):
    return (row // 2 + 2 * (row % 2) + column // 4 + column % 4) % 4


def column_slot(row, column):
    return (row % 2) * 6 + (row // 8) * 3 + share(row, column) - 1


def row_slot(row, column):
    return (column // 4) * 3 + share(row, column) - 1


def row_slot_by_parity(row, column):
    z = column // 4
    return (z % 2) * 12 + (z // 2) * 3 + share(row, column) - 1


def ring_8(k):
    return jnp.where(k % 2 == 1, (k + 1) // 2, (8 - k // 2) % 8)


def ring_4(k):
    return jnp.where(k == 2, 3, jnp.where(k == 3, 2, k))


def make_units(core, wave, table, keep, good, spec, mag, turn, sent):
    @pl.loop(0, 2)
    def _(half):
        cols = pl.ds(pl.multiple_of(half * 256, 256), 256)
        spec[:, cols] = lax.dot_general(
            table[...], wave[cols, :], (((1,), (1,)), ((), ())), preferred_element_type=F32
        )

    def add_magnitude(g, total):
        at = pl.multiple_of(g * 8, 8)
        re = spec[pl.ds(at, 8), :]
        im = spec[pl.ds(pl.multiple_of(BINS + at, 8), 8), :]
        m = jnp.sqrt(re * re + im * im)
        mag[pl.ds(at, 8), :] = m
        return total + m

    total = lax.fori_loop(0, BINS // 8, add_magnitude, jnp.zeros((8, 512), F32), unroll=4)
    water = 0.5 * (jnp.sum(total, axis=0, keepdims=True) * (1.0 / BINS)) + 1e-06
    good_f = good[...].astype(F32)
    good_2 = jnp.concatenate([good_f, good_f], axis=1)
    lower = lax.broadcasted_iota(jnp.int32, (1, 128), 1) < 64
    flags = jnp.concatenate(
        [good_2 * jnp.where(lower, keep[2 * t].astype(F32), keep[2 * t + 1].astype(F32)) for t in range(4)], axis=1
    )
    lower8 = lax.broadcasted_iota(jnp.int32, (8, 128), 1) < 64

    def whiten_8(at):
        weight = flags / jnp.maximum(mag[pl.ds(at, 8), :], water)
        re = spec[pl.ds(at, 8), :] * weight
        im = spec[pl.ds(pl.multiple_of(BINS + at, 8), 8), :] * weight
        rows = pl.multiple_of(at * 8, 64)
        for t in range(4):
            r_t, i_t = re[:, 128 * t : 128 * t + 128], im[:, 128 * t : 128 * t + 128]
            turn[pl.ds(rows + 2 * t, 8, stride=8), :] = jnp.where(lower8, r_t, pltpu.roll(i_t, 64, 1))
            turn[pl.ds(rows + 2 * t + 1, 8, stride=8), :] = jnp.where(lower8, pltpu.roll(r_t, 64, 1), i_t)

    def put(at, k, place):
        sent[place] = turn[pl.ds(pl.multiple_of(at * 8 + 8 * k, 8), 8), :].astype(BF16)

    on_0 = core == 0

    @pl.loop(0, 8)
    def _(y0):
        for block in range(3):
            at = pl.multiple_of(y0 * 24 + 8 * block, 8)
            whiten_8(at)
            for k in range(8):
                slot = 8 * block + k
                z0, r0 = slot // 3, slot % 3
                x0 = (r0 + 1 - z0 + 32 - y0) % 4
                place_0 = x0 * 12 + (y0 // 4) * 3 + (z0 * 48 + r0)
                place_1 = y0 * 48 + ((z0 % 2) * 12 + (z0 // 2) * 3 + r0)
                put(at, k, jnp.where(on_0, place_0, place_1))

    @pl.loop(0, 8)
    def _(z1):
        for block in range(3):
            at = pl.multiple_of(192 + z1 * 24 + 8 * block, 8)
            whiten_8(at)
            for k in range(8):
                x1, slot = (8 * block + k) // 6, (8 * block + k) % 6
                yh1, r1 = slot // 3, slot % 3
                yl1 = (r1 + 1 - 2 - x1 + 32 - z1) % 4
                place_0 = z1 * 48 + (x1 * 12 + 6 + slot)
                place_1 = yl1 * 48 + (z1 % 2) * 12 + (z1 // 2) * 3 + (yh1 * 192 + 24 + r1)
                put(at, k, jnp.where(on_0, place_0, place_1))


def gather_blocks(got, gram_in):
    for c in range(2):
        for yl in range(4):
            block = got[c, 2 * yl : 2 * yl + 2].astype(F32).reshape(512, 128).astype(BF16)
            gram_in[:, 128 * (4 * c + yl) : 128 * (4 * c + yl) + 128] = block


def block_of(chan):
    return (chan % 2) * 4 + chan // 2


def cross_of(core, chans, gram_in, cross):
    sign = jnp.where(lax.broadcasted_iota(jnp.int32, (1, 128), 1) < 64, 1.0, -1.0).astype(F32)
    b_ids = lax.broadcasted_iota(jnp.int32, (64, 128), 0)
    a_ids = lax.broadcasted_iota(jnp.int32, (64, 128), 1) % 64
    same = b_ids == a_ids
    ids = [block_of(chan) for chan in chans]
    left = jnp.concatenate(
        [gram_in[:, pl.ds(pl.multiple_of(i * 128, 128), 128)] for i in ids], axis=1
    )
    products = lax.dot_general(left, gram_in[...], (((0,), (0,)), ((), ())), preferred_element_type=F32)
    for second in range(2):
        seg_b = chans[second] * 8
        to_y, to_column = (seg_b // 32) * 4, seg_b % 32
        base = jnp.where(core == 0, to_column * 16 + to_y * 2, to_y * 64 + to_column)
        step_part = jnp.where(core == 0, 16, 1)
        step_row = jnp.where(core == 0, 1, 32)
        for j in range(8):
            tile = products[128 * second : 128 * second + 128, 128 * j : 128 * j + 128]
            summed = tile[:64] + sign * pltpu.roll(tile[64:], 64, 1)
            summed = jnp.where(jnp.logical_and(same, ids[second] == j), 0.0, summed)
            chan_a = (j % 4) * 2 + j // 4
            at = base + step_row * chan_a
            for part in range(8):
                cross[at + step_part * part] = summed[8 * part : 8 * part + 8].astype(BF16)


def make_lhs(done_a, done_b, rows_f, lhs_f, lhs_out):
    rows_f[0:1536] = done_a[...].astype(F32).reshape(1536, 128)
    rows_f[1536:3072] = done_b[...].astype(F32).reshape(1536, 128)
    for b in range(8):
        turned = rows_f[pl.ds(b, BINS, stride=8), :].T
        for p in range(2):
            for k in range(3):
                lhs_f[3 * p + k, pl.ds(b, 64, stride=8), :] = turned[64 * p : 64 * p + 64, 128 * k : 128 * k + 128]
    for k in range(6):
        lhs_out[:, 128 * k : 128 * k + 128] = lhs_f[k].astype(BF16)


def stack_kernel(
    wave_hbm, table_hbm, keep_hbm, good_hbm, lhs_out,
    wave, table, keep, good,
    spec, mag, turn, sent, mid_a, mid_b, got, gram_in, cross, back_a, back_b, done_a, done_b, rows_f, lhs_f,
    send_sem, recv_sem, local_sem, load_sem,
):
    chan = lax.axis_index("chan")
    seg = lax.axis_index("seg")
    core = chan % 2
    y = (seg // 32) * 4 + chan // 2
    column = seg % 32
    z, x = column // 4, column % 4
    row = y * 2 + core
    y8 = (chan // 2) * 2 + seg // 32
    owner = share(row, column) != 0

    loads = [
        pltpu.make_async_copy(src, dst, load_sem.at[n])
        for n, (src, dst) in enumerate(((table_hbm, table), (wave_hbm, wave), (keep_hbm, keep), (good_hbm, good)))
    ]
    for load in loads:
        load.start()

    def next_column(k):
        k = 32 - k
        return ((z + ring_8(k % 8)) % 8) * 4 + (x + ring_4(k // 8)) % 4

    def next_row(k):
        k = 16 - k
        return ((y + ring_8(k % 8)) % 8) * 2 + (core + k // 8) % 2

    barrier = pltpu.get_barrier_semaphore()

    @pl.loop(1, 32)
    def _(k):
        pl.semaphore_signal(barrier, inc=1, device_id=device_of(row, next_column(k)), device_id_type=MESH)

    @pl.loop(1, 16)
    def _(k):
        pl.semaphore_signal(barrier, inc=1, device_id=device_of(next_row(k), column), device_id_type=MESH)

    def remote(src, dst, n, m, to_row, to_column):
        return pltpu.make_async_remote_copy(
            src_ref=src, dst_ref=dst, send_sem=send_sem.at[n], recv_sem=recv_sem.at[m],
            device_id=device_of(to_row, to_column), device_id_type=MESH,
        )

    def local(src, dst, n):
        return pltpu.make_async_copy(src, dst, local_sem.at[n])

    def wait_bytes(ref, sem):
        pltpu.make_async_copy(ref, ref, sem).wait()

    for load in loads:
        load.wait()
    make_units(core, wave, table, keep, good, spec, mag, turn, sent)

    pl.semaphore_wait(barrier, 46)

    @pl.when(core == 0)
    def _():
        local(sent.at[pl.ds(column * 12, 12)], mid_a.at[column], 0).start()
        for c in range(2):
            @pl.loop(1, 32)
            def _(k):
                to = next_column(k)
                remote(sent.at[pl.ds(to * 12 + 6 * c, 6)], mid_a.at[column, pl.ds(6 * c, 6)], 0, c, row, to).start()

    @pl.when(core == 1)
    def _():
        local(sent.at[pl.ds(row * 24, 24)], mid_b.at[y8], 1).start()
        for c in range(2):
            @pl.loop(1, 16)
            def _(k):
                to = next_row(k)
                remote(sent.at[pl.ds(to * 24 + 12 * c, 12)], mid_b.at[y8, pl.ds(12 * c, 12)], 1, 2 + c, to, column).start()

    @pl.when(core == 0)
    def _():
        wait_bytes(mid_a.at[0], local_sem.at[0])

    @pl.when(core == 1)
    def _():
        wait_bytes(mid_b.at[0], local_sem.at[1])

    for c in range(2):
        @pl.when(core == 0)
        def _():
            wait_bytes(mid_a.at[pl.ds(0, 31), pl.ds(0, 6)], recv_sem.at[c])

            @pl.loop(0, 8)
            def _(k):
                to = ((y + ring_8(7 - k)) % 8) * 2 + c

                @pl.when(jnp.logical_and(share(to, column) != 0, to != row))
                def _():
                    remote(mid_a.at[:, column_slot(to, column)], got.at[0, y8], 2, 4, to, column).start()

            wait_bytes(mid_b.at[:, pl.ds(0, 12)], recv_sem.at[2 + c])

        @pl.when(core == 1)
        def _():
            wait_bytes(mid_b.at[pl.ds(0, 7), pl.ds(0, 12)], recv_sem.at[2 + c])

        @pl.loop(0, 16)
        def _(k):
            back = 15 - k
            to = ((z + (z + c) % 2 + 2 * ring_4(back % 4)) % 8) * 4 + (x + ring_4(back // 4)) % 4

            @pl.when(jnp.logical_and(share(row, to) != 0, to != column))
            def _():
                remote(mid_b.at[:, row_slot_by_parity(row, to)], got.at[1, :, column], 3, 5, row, to).start()

    @pl.when(owner)
    def _():
        @pl.when(core == 0)
        def _():
            local(mid_a.at[:, column_slot(row, column)], got.at[0, y8], 2).start()

        local(mid_b.at[:, row_slot_by_parity(row, column)], got.at[1, :, column], 3).start()
        wait_bytes(got.at[1, :, 0], local_sem.at[3])
        wait_bytes(got.at[1, :, pl.ds(0, 31)], recv_sem.at[5])

        @pl.when(core == 0)
        def _():
            wait_bytes(got.at[0, 0], local_sem.at[2])
            wait_bytes(got.at[0, pl.ds(0, 7)], recv_sem.at[4])

        @pl.when(core == 1)
        def _():
            wait_bytes(got.at[0], recv_sem.at[4])

        gather_blocks(got, gram_in)
        slot_a = row_slot(row, column)
        slot_b = column_slot(row, column) % 6

        @pl.loop(0, 4)
        def _(quarter):
            pair = (quarter + z // 2) % 4
            part = (quarter + 2 * (1 - y // 4)) % 4
            first = jnp.where(core == 0, pair, 2 * part)
            second = jnp.where(core == 0, pair + 4, 2 * part + 1)
            cross_of(core, (first, second), gram_in, cross)

            @pl.when(core == 0)
            def _():
                @pl.loop(0, 8)
                def _(k):
                    to = pair * 8 + (column + k + 1) % 8

                    @pl.when(to != column)
                    def _():
                        remote(cross.at[pl.ds(to * 16, 16)], back_a.at[slot_a], 4, 6, row, to).start()

                    @pl.when(to == column)
                    def _():
                        local(cross.at[pl.ds(to * 16, 16)], back_a.at[slot_a], 4).start()

            @pl.when(core == 1)
            def _():
                half = (part % 2) * 16

                @pl.loop(0, 8)
                def _(k):
                    to = (part // 2) * 8 + (row + k + 1) % 8

                    @pl.when(to != row)
                    def _():
                        remote(
                            cross.at[pl.ds(to * 32 + half, 16)], back_b.at[slot_b, pl.ds(half, 16)], 5, 7, to, column
                        ).start()

                    @pl.when(to == row)
                    def _():
                        local(cross.at[pl.ds(to * 32 + half, 16)], back_b.at[slot_b, pl.ds(half, 16)], 5).start()

    @pl.when(core == 0)
    def _():
        @pl.when(owner)
        def _():
            wait_bytes(back_a.at[0], local_sem.at[4])
            wait_bytes(back_a.at[pl.ds(0, 23)], recv_sem.at[6])

        @pl.when(jnp.logical_not(owner))
        def _():
            wait_bytes(back_a, recv_sem.at[6])

        @pl.loop(1, 16)
        def _(k):
            to = next_row(k)
            remote(back_a.at[:, to], done_a.at[y], 6, 8, to, column).start()

        local(back_a.at[:, row], done_a.at[y], 6).start()

    own_back = jnp.logical_and(owner, core == 1)

    @pl.when(own_back)
    def _():
        wait_bytes(back_b.at[0], local_sem.at[5])
        wait_bytes(back_b.at[pl.ds(0, 5)], recv_sem.at[7])

    @pl.when(jnp.logical_not(own_back))
    def _():
        wait_bytes(back_b, recv_sem.at[7])

    @pl.loop(1, 32)
    def _(k):
        to = next_column(k)
        remote(back_b.at[:, to], done_b.at[column], 7, 9, row, to).start()

    local(back_b.at[:, column], done_b.at[column], 7).start()

    @pl.when(core == 0)
    def _():
        wait_bytes(done_a.at[0], local_sem.at[6])
        wait_bytes(done_a.at[pl.ds(0, 7)], recv_sem.at[8])

    @pl.when(core == 1)
    def _():
        wait_bytes(done_a, recv_sem.at[8])

    wait_bytes(done_b.at[0], local_sem.at[7])
    wait_bytes(done_b.at[pl.ds(0, 31)], recv_sem.at[9])
    make_lhs(done_a, done_b, rows_f, lhs_f, lhs_out)

    @pl.when(core == 0)
    def _():
        wait_bytes(mid_a.at[pl.ds(0, 31)], send_sem.at[0])

        @pl.when(owner)
        def _():
            wait_bytes(got.at[0, pl.ds(0, 8)], send_sem.at[2])
            wait_bytes(got.at[0, pl.ds(0, 3)], send_sem.at[2])
            wait_bytes(cross.at[pl.ds(0, 31 * 16)], send_sem.at[4])

        @pl.when(jnp.logical_not(owner))
        def _():
            wait_bytes(got.at[0, pl.ds(0, 8)], send_sem.at[2])
            wait_bytes(got.at[0, pl.ds(0, 4)], send_sem.at[2])

        wait_bytes(done_a.at[pl.ds(0, 8)], send_sem.at[6])
        wait_bytes(done_a.at[pl.ds(0, 7)], send_sem.at[6])

    @pl.when(core == 1)
    def _():
        wait_bytes(sent.at[pl.ds(0, 15 * 24)], send_sem.at[1])

        @pl.when(owner)
        def _():
            wait_bytes(cross.at[pl.ds(0, 15 * 32)], send_sem.at[5])

    @pl.when(owner)
    def _():
        wait_bytes(got.at[1, :, pl.ds(0, 23)], send_sem.at[3])

    @pl.when(jnp.logical_not(owner))
    def _():
        wait_bytes(got.at[1, :, pl.ds(0, 24)], send_sem.at[3])

    wait_bytes(done_b.at[pl.ds(0, 31)], send_sem.at[7])


def stacked(wave, table, keep, good):
    anywhere = pl.BlockSpec(memory_space=pl.ANY)
    return pl.pallas_call(
        stack_kernel,
        out_shape=jax.ShapeDtypeStruct((512, 2 * BINS), BF16),
        in_specs=[anywhere] * 4,
        out_specs=pl.BlockSpec(memory_space=pltpu.VMEM),
        scratch_shapes=[
            pltpu.VMEM((512, NT), BF16),
            pltpu.VMEM((2 * BINS, NT), BF16),
            pltpu.SMEM((8,), jnp.int32),
            pltpu.VMEM((1, 64), jnp.int32),
            pltpu.VMEM((2 * BINS, 512), F32),
            pltpu.VMEM((BINS, 512), F32),
            pltpu.VMEM((BINS * 8, 128), F32),
            pltpu.VMEM((BINS, 8, 128), BF16),
            pltpu.VMEM((32, 12, 8, 128), BF16),
            pltpu.VMEM((8, 24, 8, 128), BF16),
            pltpu.VMEM((2, 8, 32, 8, 128), BF16),
            pltpu.VMEM((512, 1024), BF16),
            pltpu.VMEM((512, 8, 128), BF16),
            pltpu.VMEM((24, 16, 8, 128), BF16),
            pltpu.VMEM((6, 32, 8, 128), BF16),
            pltpu.VMEM((8, 24, 8, 128), BF16),
            pltpu.VMEM((32, 6, 8, 128), BF16),
            pltpu.VMEM((3072, 128), F32),
            pltpu.VMEM((6, 512, 128), F32),
            pltpu.SemaphoreType.DMA((8,)),
            pltpu.SemaphoreType.DMA((10,)),
            pltpu.SemaphoreType.DMA((8,)),
            pltpu.SemaphoreType.DMA((4,)),
        ],
        compiler_params=pltpu.CompilerParams(collective_id=0, has_side_effects=True, vmem_limit_bytes=48 << 20),
        name="stack_cross_spectra",
    )(wave, table, keep, good)


def lag_kernel(scale, lhs, table, out, block, sem):
    width = block.shape[-1]
    count = LAGS // width
    for n in range(count):
        if n >= 2:
            pltpu.make_async_copy(block.at[n % 2], out.at[:, :, pl.ds((n - 2) * width, width)], sem.at[n % 2]).wait()
        values = jnp.dot(lhs[...], table[:, n * width : (n + 1) * width], preferred_element_type=F32) * scale
        block[n % 2] = values.reshape(64, 8, width).astype(BF16)
        pltpu.make_async_copy(block.at[n % 2], out.at[:, :, pl.ds(n * width, width)], sem.at[n % 2]).start()
    for n in range(count - 2, count):
        pltpu.make_async_copy(block.at[n % 2], out.at[:, :, pl.ds(n * width, width)], sem.at[n % 2]).wait()


def lagged(lhs, table, scale):
    vmem = pl.BlockSpec(memory_space=pltpu.VMEM)
    return pl.pallas_call(
        functools.partial(lag_kernel, scale),
        out_shape=jax.ShapeDtypeStruct((64, 8, LAGS), BF16),
        in_specs=[vmem, vmem],
        out_specs=pl.BlockSpec(memory_space=pl.ANY),
        scratch_shapes=[pltpu.VMEM((2, 64, 8, 512), BF16), pltpu.SemaphoreType.DMA((2,))],
        compiler_params=pltpu.CompilerParams(vmem_limit_bytes=48 << 20),
        name="lag_transform",
    )(lhs, table)


def local(waveforms, segment_keep, channel_good):
    wave = waveforms.reshape(512, NT)
    lhs = stacked(wave, jnp.asarray(forward_rows()), segment_keep, channel_good.reshape(1, 64))
    return lagged(lhs, jnp.asarray(lag_rows()), float(1.0 / np.sqrt(SEGS * BINS)))


def solution(mesh):
    placed = (P("seg", "chan", None), P("seg"), P("chan"))
    return jax.shard_map(
        local, mesh=mesh, in_specs=placed, out_specs=P("chan", "seg", None), check_vma=False
    )
```

time: 101 us -> 77.1 us (0.76)
  Pallas kernels: 96.5 us -> 72.4 us
    pallas_call x1, Pallas kernels: 92.2 us -> 68.2 us  [stacked(): pl.pallas_call(stack_kernel, out_shape=jax.ShapeDtypeStruct((512, 2 * BIN...]
where the time goes in v1:
time: 77.1 us; the launch traced here: 77 us
  Pallas kernels  72.4 us (94%)
  local copies, waits for them, and re-layouts  4.61 us (6%)
    pallas_call x1, Pallas kernels, stacked(): pl.pallas_call(stack_kernel, out_shape=jax.ShapeDtypeStruct((512, 2 * BIN...  68.2 us
    unnamed x10, local copies, waits for them, and re-layouts  4.61 us
    pallas_call x1, Pallas kernels, lagged(): pl.pallas_call(functools.partial(lag_kernel, scale), out_shape=jax.ShapeD...  4.12 us

profile of v1, /device:TPU:1, one launch (start us, length us, event | category | flops | bytes accessed | tf_op | source)
XLA Modules:
  0.0 77.0 jit_solution(12341821920999142895)
XLA Ops:
  0.0 0.0 copy-start
  0.0 0.0 copy-start.1
  0.0 1.8 %copy-done.1 = bf16[768,1536]{1,0:T(8,128)(2,1)S(1)} copy-done((bf16[768,1536]{1,0:T(8,128)(2,1)S(1)}, bf16[768,1536]{1,0:T(8,128)(2,1)}, u32[]{:S(2)}) %copy-start.1) | copy-done | bytes 2359320
  1.8 0.0 copy-start.2
  1.8 1.5 %copy-done.2 = bf16[8,64,1536]{2,1,0:T(8,128)(2,1)S(1)} copy-done((bf16[8,64,1536]{2,1,0:T(8,128)(2,1)S(1)}, bf16[8,64,1536]{2,1,0:T(8,128)(2,1)}, u32[]{:S(2)}) %copy-start.2) | copy-done | bytes 1572888
  3.3 0.0 copy-start.3
  3.3 0.7 copy-done.3
  4.0 0.0 copy-start.4
  4.0 0.7 copy-done.4
  4.6 68.2 %stack_cross_spectra.1.lhs = bf16[512,768]{1,0:T(8,128)(2,1)S(1)} custom-call(bf16[512,1536]{1,0:T(8,128)(2,1)S(1)} %bitcast.2, bf16[768,1536]{1,0:T(8,128)(2,1)S(1)} %copy-done.1, s32[8]{0:T(128)S(1)} %copy-done.3, s32[1,64]{1,0:T(1,128)S(1)} %bitcast.3), custom_call_target="tpu_custom_call" | custom-call | tf_op jit(solution)/shard_map/stack_cross_spectra/pallas_call | solution.py:451
  72.9 0.0 copy-done
  72.9 4.1 %lag_transform.1 = bf16[64,8,2560]{2,1,0:T(8,128)(2,1)} custom-call(bf16[512,768]{1,0:T(8,128)(2,1)S(1)} %stack_cross_spectra.1.lhs, bf16[768,2560]{1,0:T(8,128)(2,1)S(1)} %copy-done), custom_call_target="tpu_custom_call" | custom-call | tf_op jit(solution)/shard_map/lag_transform/pallas_call | solution.py:501
Async XLA Ops:
  0.0 72.9 %copy-start = (bf16[768,2560]{1,0:T(8,128)(2,1)S(1)}, bf16[768,2560]{1,0:T(8,128)(2,1)}, u32[]{:S(2)}) copy-start(bf16[768,2560]{1,0:T(8,128)(2,1)} %constant.5.clone.table) | copy-start | bytes 11796484
  0.0 1.8 %copy-start.1 = (bf16[768,1536]{1,0:T(8,128)(2,1)S(1)}, bf16[768,1536]{1,0:T(8,128)(2,1)}, u32[]{:S(2)}) copy-start(bf16[768,1536]{1,0:T(8,128)(2,1)} %constant.4.clone.table_hbm) | copy-start | bytes 7077892
  1.8 1.5 %copy-start.2 = (bf16[8,64,1536]{2,1,0:T(8,128)(2,1)S(1)}, bf16[8,64,1536]{2,1,0:T(8,128)(2,1)}, u32[]{:S(2)}) copy-start(bf16[8,64,1536]{2,1,0:T(8,128)(2,1)} %param.5) | copy-start | bytes 4718596
  3.3 0.7 copy-start.3
  4.0 0.7 copy-start.4

commit v2 on v1

--- a/solution.py
+++ b/solution.py
@@ -59,6 +59,10 @@
     return (z % 2) * 12 + (z // 2) * 3 + share(row, column) - 1
 
 
+def turned_column(column):
+    return ((column // 8) % 2) * 16 + (column // 16) * 8 + column % 8
+
+
 def ring_8(k):
     return jnp.where(k % 2 == 1, (k + 1) // 2, (8 - k // 2) % 8)
 
@@ -67,12 +71,13 @@
     return jnp.where(k == 2, 3, jnp.where(k == 3, 2, k))
 
 
-def make_units(core, wave, table, keep, good, spec, mag, turn, sent):
-    @pl.loop(0, 2)
-    def _(half):
-        cols = pl.ds(pl.multiple_of(half * 256, 256), 256)
-        spec[:, cols] = lax.dot_general(
-            table[...], wave[cols, :], (((1,), (1,)), ((), ())), preferred_element_type=F32
+def make_units(core, wave, table, keep, good, spec, mag, turn, sent, loaded=None, between=None):
+    for third in range(3):
+        if loaded is not None:
+            loaded(third)
+        rows = slice(256 * third, 256 * third + 256)
+        spec[rows, :] = lax.dot_general(
+            table[rows, :], wave[...], (((1,), (1,)), ((), ())), preferred_element_type=F32
         )
 
     def add_magnitude(g, total):
@@ -121,6 +126,9 @@
                 place_1 = y0 * 48 + ((z0 % 2) * 12 + (z0 // 2) * 3 + r0)
                 put(at, k, jnp.where(on_0, place_0, place_1))
 
+    if between is not None:
+        between()
+
     @pl.loop(0, 8)
     def _(z1):
         for block in range(3):
@@ -135,11 +143,10 @@
                 put(at, k, jnp.where(on_0, place_0, place_1))
 
 
-def gather_blocks(got, gram_in):
-    for c in range(2):
-        for yl in range(4):
-            block = got[c, 2 * yl : 2 * yl + 2].astype(F32).reshape(512, 128).astype(BF16)
-            gram_in[:, 128 * (4 * c + yl) : 128 * (4 * c + yl) + 128] = block
+def gather_blocks(c, got, gram_in):
+    for yl in range(4):
+        block = got[c, 2 * yl : 2 * yl + 2].astype(F32).reshape(512, 128).astype(BF16)
+        gram_in[:, 128 * (4 * c + yl) : 128 * (4 * c + yl) + 128] = block
 
 
 def block_of(chan):
@@ -157,9 +164,9 @@
     )
     products = lax.dot_general(left, gram_in[...], (((0,), (0,)), ((), ())), preferred_element_type=F32)
     for second in range(2):
-        seg_b = chans[second] * 8
-        to_y, to_column = (seg_b // 32) * 4, seg_b % 32
-        base = jnp.where(core == 0, to_column * 16 + to_y * 2, to_y * 64 + to_column)
+        chan_b = chans[second]
+        to_y, to_column = (chan_b // 4) * 4, (chan_b % 4) * 8
+        base = jnp.where(core == 0, to_column * 16 + to_y * 2, to_y * 64 + turned_column(to_column))
         step_part = jnp.where(core == 0, 16, 1)
         step_row = jnp.where(core == 0, 1, 32)
         for j in range(8):
@@ -172,8 +179,12 @@
                 cross[at + step_part * part] = summed[8 * part : 8 * part + 8].astype(BF16)
 
 
-def make_lhs(done_a, done_b, rows_f, lhs_f, lhs_out):
-    rows_f[0:1536] = done_a[...].astype(F32).reshape(1536, 128)
+def make_lhs(z_pair, done_a, done_b, rows_f, lhs_f, lhs_out):
+    for quarter in range(4):
+        of_pair = (z_pair + 4 - quarter) % 4
+        for y in range(8):
+            values = done_a[y, 6 * quarter : 6 * quarter + 6].astype(F32).reshape(48, 128)
+            rows_f[pl.ds(pl.multiple_of(of_pair * 48 + y * 192, 16), 48), :] = values
     rows_f[1536:3072] = done_b[...].astype(F32).reshape(1536, 128)
     for b in range(8):
         turned = rows_f[pl.ds(b, BINS, stride=8), :].T
@@ -200,9 +211,13 @@
     y8 = (chan // 2) * 2 + seg // 32
     owner = share(row, column) != 0
 
+    thirds = [pl.ds(256 * n, 256) for n in range(3)]
     loads = [
         pltpu.make_async_copy(src, dst, load_sem.at[n])
-        for n, (src, dst) in enumerate(((table_hbm, table), (wave_hbm, wave), (keep_hbm, keep), (good_hbm, good)))
+        for n, (src, dst) in enumerate(
+            ((wave_hbm, wave), (table_hbm.at[thirds[0]], table.at[thirds[0]]), (keep_hbm, keep), (good_hbm, good),
+             (table_hbm.at[thirds[1]], table.at[thirds[1]]), (table_hbm.at[thirds[2]], table.at[thirds[2]]))
+        )
     ]
     for load in loads:
         load.start()
@@ -237,29 +252,49 @@
     def wait_bytes(ref, sem):
         pltpu.make_async_copy(ref, ref, sem).wait()
 
-    for load in loads:
-        load.wait()
-    make_units(core, wave, table, keep, good, spec, mag, turn, sent)
-
-    pl.semaphore_wait(barrier, 46)
+    def loaded(third):
+        for n in ((0, 1, 2, 3), (4,), (5,))[third]:
+            loads[n].wait()
+
+    def to_columns(c):
+        @pl.loop(1, 32)
+        def _(k):
+            to = next_column(k)
+            remote(sent.at[pl.ds(to * 12 + 6 * c, 6)], mid_a.at[column, pl.ds(6 * c, 6)], 0, c, row, to).start()
+
+    def to_rows(c, to_core):
+        @pl.loop(0, 8)
+        def _(k):
+            to = ((y + ring_8(7 - k)) % 8) * 2 + to_core
+
+            @pl.when(to != row)
+            def _():
+                remote(sent.at[pl.ds(to * 24 + 12 * c, 12)], mid_b.at[y8, pl.ds(12 * c, 12)], 1, 2 + c, to, column).start()
+
+    def first_sends():
+        pl.semaphore_wait(barrier, 46)
+
+        @pl.when(core == 0)
+        def _():
+            to_columns(0)
+
+        @pl.when(core == 1)
+        def _():
+            to_rows(0, 0)
+
+    make_units(core, wave, table, keep, good, spec, mag, turn, sent, loaded, first_sends)
 
     @pl.when(core == 0)
     def _():
+        to_columns(1)
         local(sent.at[pl.ds(column * 12, 12)], mid_a.at[column], 0).start()
-        for c in range(2):
-            @pl.loop(1, 32)
-            def _(k):
-                to = next_column(k)
-                remote(sent.at[pl.ds(to * 12 + 6 * c, 6)], mid_a.at[column, pl.ds(6 * c, 6)], 0, c, row, to).start()
 
     @pl.when(core == 1)
     def _():
+        to_rows(0, 1)
+        to_rows(1, 0)
+        to_rows(1, 1)
         local(sent.at[pl.ds(row * 24, 24)], mid_b.at[y8], 1).start()
-        for c in range(2):
-            @pl.loop(1, 16)
-            def _(k):
-                to = next_row(k)
-                remote(sent.at[pl.ds(to * 24 + 12 * c, 12)], mid_b.at[y8, pl.ds(12 * c, 12)], 1, 2 + c, to, column).start()
 
     @pl.when(core == 0)
     def _():
@@ -304,28 +339,29 @@
             local(mid_a.at[:, column_slot(row, column)], got.at[0, y8], 2).start()
 
         local(mid_b.at[:, row_slot_by_parity(row, column)], got.at[1, :, column], 3).start()
+        @pl.when(core == 0)
+        def _():
+            wait_bytes(got.at[0, 0], local_sem.at[2])
+            wait_bytes(got.at[0, pl.ds(0, 7)], recv_sem.at[4])
+
+        @pl.when(core == 1)
+        def _():
+            wait_bytes(got.at[0], recv_sem.at[4])
+
+        gather_blocks(0, got, gram_in)
         wait_bytes(got.at[1, :, 0], local_sem.at[3])
         wait_bytes(got.at[1, :, pl.ds(0, 31)], recv_sem.at[5])
-
-        @pl.when(core == 0)
-        def _():
-            wait_bytes(got.at[0, 0], local_sem.at[2])
-            wait_bytes(got.at[0, pl.ds(0, 7)], recv_sem.at[4])
-
-        @pl.when(core == 1)
-        def _():
-            wait_bytes(got.at[0], recv_sem.at[4])
-
-        gather_blocks(got, gram_in)
-        slot_a = row_slot(row, column)
+        gather_blocks(1, got, gram_in)
+
+        slot_a = row_slot(row, column) % 6
         slot_b = column_slot(row, column) % 6
 
         @pl.loop(0, 4)
         def _(quarter):
             pair = (quarter + z // 2) % 4
-            part = (quarter + 2 * (1 - y // 4)) % 4
-            first = jnp.where(core == 0, pair, 2 * part)
-            second = jnp.where(core == 0, pair + 4, 2 * part + 1)
+            to_hi, half = (quarter // 2 + 1 - y // 4) % 2, quarter % 2
+            first = jnp.where(core == 0, pair, to_hi * 4 + half)
+            second = jnp.where(core == 0, pair + 4, to_hi * 4 + half + 2)
             cross_of(core, (first, second), gram_in, cross)
 
             @pl.when(core == 0)
@@ -333,81 +369,95 @@
                 @pl.loop(0, 8)
                 def _(k):
                     to = pair * 8 + (column + k + 1) % 8
+                    slot = quarter * 6 + slot_a
 
                     @pl.when(to != column)
                     def _():
-                        remote(cross.at[pl.ds(to * 16, 16)], back_a.at[slot_a], 4, 6, row, to).start()
+                        remote(cross.at[pl.ds(to * 16, 16)], back_a.at[slot], 4, 6 + quarter // 2, row, to).start()
 
                     @pl.when(to == column)
                     def _():
-                        local(cross.at[pl.ds(to * 16, 16)], back_a.at[slot_a], 4).start()
+                        local(cross.at[pl.ds(to * 16, 16)], back_a.at[slot], 4).start()
 
             @pl.when(core == 1)
             def _():
-                half = (part % 2) * 16
-
                 @pl.loop(0, 8)
                 def _(k):
-                    to = (part // 2) * 8 + (row + k + 1) % 8
+                    to = to_hi * 8 + (row + k + 1) % 8
+                    src = cross.at[pl.ds(to * 32 + half * 16, 16)]
+                    dst = back_b.at[slot_b, pl.ds(half * 16, 16)]
 
                     @pl.when(to != row)
                     def _():
-                        remote(
-                            cross.at[pl.ds(to * 32 + half, 16)], back_b.at[slot_b, pl.ds(half, 16)], 5, 7, to, column
-                        ).start()
+                        remote(src, dst, 5, 8 + half, to, column).start()
 
                     @pl.when(to == row)
                     def _():
-                        local(cross.at[pl.ds(to * 32 + half, 16)], back_b.at[slot_b, pl.ds(half, 16)], 5).start()
+                        local(src, dst, 5).start()
+
+    own_a = jnp.logical_and(owner, core == 0)
+    own_b = jnp.logical_and(owner, core == 1)
+
+    @pl.when(own_b)
+    def _():
+        wait_bytes(back_b.at[0], local_sem.at[5])
+
+    for c in range(2):
+        @pl.when(core == 0)
+        def _():
+            if c == 0:
+                @pl.when(own_a)
+                def _():
+                    wait_bytes(back_a.at[0], local_sem.at[4])
+                    wait_bytes(back_a.at[pl.ds(0, 11)], recv_sem.at[6])
+
+                @pl.when(jnp.logical_not(own_a))
+                def _():
+                    wait_bytes(back_a.at[pl.ds(0, 12)], recv_sem.at[6])
+            else:
+                wait_bytes(back_a.at[pl.ds(0, 12)], recv_sem.at[7])
+
+            @pl.loop(1, 16)
+            def _(k):
+                to = next_row(k)
+                slots = pl.ds(12 * c, 12)
+                remote(back_a.at[slots, to], done_a.at[y, slots], 6, 10, to, column).start()
+
+        @pl.when(own_b)
+        def _():
+            wait_bytes(back_b.at[pl.ds(0, 5), pl.ds(0, 16)], recv_sem.at[8 + c])
+
+        @pl.when(jnp.logical_not(own_b))
+        def _():
+            wait_bytes(back_b.at[:, pl.ds(0, 16)], recv_sem.at[8 + c])
+
+        @pl.loop(0, 16)
+        def _(k):
+            place = (turned_column(column) + k + 1) % 16
+            to = (place // 8) * 16 + c * 8 + place % 8
+
+            @pl.when(to != column)
+            def _():
+                remote(back_b.at[:, place + 16 * c], done_b.at[column], 7, 11, row, to).start()
 
     @pl.when(core == 0)
     def _():
-        @pl.when(owner)
-        def _():
-            wait_bytes(back_a.at[0], local_sem.at[4])
-            wait_bytes(back_a.at[pl.ds(0, 23)], recv_sem.at[6])
-
-        @pl.when(jnp.logical_not(owner))
-        def _():
-            wait_bytes(back_a, recv_sem.at[6])
-
-        @pl.loop(1, 16)
-        def _(k):
-            to = next_row(k)
-            remote(back_a.at[:, to], done_a.at[y], 6, 8, to, column).start()
-
         local(back_a.at[:, row], done_a.at[y], 6).start()
 
-    own_back = jnp.logical_and(owner, core == 1)
-
-    @pl.when(own_back)
-    def _():
-        wait_bytes(back_b.at[0], local_sem.at[5])
-        wait_bytes(back_b.at[pl.ds(0, 5)], recv_sem.at[7])
-
-    @pl.when(jnp.logical_not(own_back))
-    def _():
-        wait_bytes(back_b, recv_sem.at[7])
-
-    @pl.loop(1, 32)
-    def _(k):
-        to = next_column(k)
-        remote(back_b.at[:, to], done_b.at[column], 7, 9, row, to).start()
-
-    local(back_b.at[:, column], done_b.at[column], 7).start()
+    local(back_b.at[:, turned_column(column)], done_b.at[column], 7).start()
 
     @pl.when(core == 0)
     def _():
         wait_bytes(done_a.at[0], local_sem.at[6])
-        wait_bytes(done_a.at[pl.ds(0, 7)], recv_sem.at[8])
+        wait_bytes(done_a.at[pl.ds(0, 7)], recv_sem.at[10])
 
     @pl.when(core == 1)
     def _():
-        wait_bytes(done_a, recv_sem.at[8])
+        wait_bytes(done_a, recv_sem.at[10])
 
     wait_bytes(done_b.at[0], local_sem.at[7])
-    wait_bytes(done_b.at[pl.ds(0, 31)], recv_sem.at[9])
-    make_lhs(done_a, done_b, rows_f, lhs_f, lhs_out)
+    wait_bytes(done_b.at[pl.ds(0, 31)], recv_sem.at[11])
+    make_lhs(z // 2, done_a, done_b, rows_f, lhs_f, lhs_out)
 
     @pl.when(core == 0)
     def _():
@@ -447,11 +497,11 @@
 
 
 def stacked(wave, table, keep, good):
-    anywhere = pl.BlockSpec(memory_space=pl.ANY)
+    in_hbm = pl.BlockSpec(memory_space=pltpu.HBM)
     return pl.pallas_call(
         stack_kernel,
         out_shape=jax.ShapeDtypeStruct((512, 2 * BINS), BF16),
-        in_specs=[anywhere] * 4,
+        in_specs=[in_hbm] * 4,
         out_specs=pl.BlockSpec(memory_space=pltpu.VMEM),
         scratch_shapes=[
             pltpu.VMEM((512, NT), BF16),
@@ -474,13 +524,13 @@
             pltpu.VMEM((3072, 128), F32),
             pltpu.VMEM((6, 512, 128), F32),
             pltpu.SemaphoreType.DMA((8,)),
-            pltpu.SemaphoreType.DMA((10,)),
+            pltpu.SemaphoreType.DMA((12,)),
             pltpu.SemaphoreType.DMA((8,)),
-            pltpu.SemaphoreType.DMA((4,)),
+            pltpu.SemaphoreType.DMA((6,)),
         ],
         compiler_params=pltpu.CompilerParams(collective_id=0, has_side_effects=True, vmem_limit_bytes=48 << 20),
         name="stack_cross_spectra",
-    )(wave, table, keep, good)
+    )(*[pltpu.with_memory_space_constraint(value, pltpu.HBM) for value in (wave, table, keep, good)])
 
 
 def lag_kernel(scale, lhs, table, out, block, sem):
@@ -503,7 +553,7 @@
         out_shape=jax.ShapeDtypeStruct((64, 8, LAGS), BF16),
         in_specs=[vmem, vmem],
         out_specs=pl.BlockSpec(memory_space=pl.ANY),
-        scratch_shapes=[pltpu.VMEM((2, 64, 8, 512), BF16), pltpu.SemaphoreType.DMA((2,))],
+        scratch_shapes=[pltpu.VMEM((2, 64, 8, LAGS // 2), BF16), pltpu.SemaphoreType.DMA((2,))],
         compiler_params=pltpu.CompilerParams(vmem_limit_bytes=48 << 20),
         name="lag_transform",
     )(lhs, table)

time: 77.1 us -> 70.3 us (0.912)
  local copies, waits for them, and re-layouts: 4.61 us -> 0.01 us
  Pallas kernels: 72.4 us -> 70.2 us
    unnamed x10 -> x2, local copies, waits for them, and re-layouts: 4.61 us -> 0.01 us
    pallas_call x1, Pallas kernels: 68.2 us -> 66.9 us  [stacked(): pl.pallas_call(stack_kernel, out_shape=jax.ShapeDtypeStruct((512, 2 * BIN...]
    pallas_call x1, Pallas kernels: 4.12 us -> 3.28 us  [lagged(): pl.pallas_call(functools.partial(lag_kernel, scale), out_shape=jax.ShapeD...]
where the time goes in v2:
time: 70.3 us; the launch traced here: 70.2 us
  Pallas kernels  70.2 us (100%)
    pallas_call x1, Pallas kernels, stacked(): pl.pallas_call(stack_kernel, out_shape=jax.ShapeDtypeStruct((512, 2 * BIN...  66.9 us
    pallas_call x1, Pallas kernels, lagged(): pl.pallas_call(functools.partial(lag_kernel, scale), out_shape=jax.ShapeD...  3.28 us

profile of v2, /device:TPU:1, one launch (start us, length us, event | category | flops | bytes accessed | tf_op | source)
XLA Modules:
  0.0 70.2 jit_solution(13933214134322305040)
XLA Ops:
  0.0 0.0 copy-start
  0.0 66.9 %stack_cross_spectra.1.lhs = bf16[512,768]{1,0:T(8,128)(2,1)S(1)} custom-call(bf16[512,1536]{1,0:T(8,128)(2,1)} %bitcast.2, bf16[768,1536]{1,0:T(8,128)(2,1)} %constant.4.clone.table_hbm, s32[8]{0:T(128)} %keep_hbm.1, s32[1,64]{1,0:T(1,128)} %bitcast.3), custom_call_target="tpu_custom_call" | custom-call | tf_op jit(solution)/shard_map/stack_cross_spectra/pallas_call | solution.py:501
  66.9 0.0 copy-done
  66.9 3.3 %lag_transform.1 = bf16[64,8,2560]{2,1,0:T(8,128)(2,1)} custom-call(bf16[512,768]{1,0:T(8,128)(2,1)S(1)} %stack_cross_spectra.1.lhs, bf16[768,2560]{1,0:T(8,128)(2,1)S(1)} %copy-done), custom_call_target="tpu_custom_call" | custom-call | tf_op jit(solution)/shard_map/lag_transform/pallas_call | solution.py:551
Async XLA Ops:
  0.0 66.9 %copy-start = (bf16[768,2560]{1,0:T(8,128)(2,1)S(1)}, bf16[768,2560]{1,0:T(8,128)(2,1)}, u32[]{:S(2)}) copy-start(bf16[768,2560]{1,0:T(8,128)(2,1)} %constant.5.clone.table) | copy-start | bytes 11796484

commit v3 on v2

--- a/solution.py
+++ b/solution.py
@@ -54,13 +54,15 @@
     return (column // 4) * 3 + share(row, column) - 1
 
 
-def row_slot_by_parity(row, column):
-    z = column // 4
-    return (z % 2) * 12 + (z // 2) * 3 + share(row, column) - 1
-
-
 def turned_column(column):
     return ((column // 8) % 2) * 16 + (column // 16) * 8 + column % 8
+
+
+QUARTERS = (2, 1, 3, 0)
+
+
+def quarter_of(step):
+    return jnp.where(step == 0, 2, jnp.where(step == 1, 1, jnp.where(step == 2, 3, 0)))
 
 
 def ring_8(k):
@@ -101,46 +103,69 @@
     def whiten_8(at):
         weight = flags / jnp.maximum(mag[pl.ds(at, 8), :], water)
         re = spec[pl.ds(at, 8), :] * weight
-        im = spec[pl.ds(pl.multiple_of(BINS + at, 8), 8), :] * weight
-        rows = pl.multiple_of(at * 8, 64)
+        im = spec[pl.ds(BINS + at, 8), :] * weight
+        rows = at * 8
         for t in range(4):
             r_t, i_t = re[:, 128 * t : 128 * t + 128], im[:, 128 * t : 128 * t + 128]
             turn[pl.ds(rows + 2 * t, 8, stride=8), :] = jnp.where(lower8, r_t, pltpu.roll(i_t, 64, 1))
             turn[pl.ds(rows + 2 * t + 1, 8, stride=8), :] = jnp.where(lower8, pltpu.roll(r_t, 64, 1), i_t)
 
-    def put(at, k, place):
-        sent[place] = turn[pl.ds(pl.multiple_of(at * 8 + 8 * k, 8), 8), :].astype(BF16)
-
-    on_0 = core == 0
-
-    @pl.loop(0, 8)
-    def _(y0):
-        for block in range(3):
-            at = pl.multiple_of(y0 * 24 + 8 * block, 8)
-            whiten_8(at)
-            for k in range(8):
-                slot = 8 * block + k
+    def whiten_half(half):
+        for block in range(24):
+            whiten_8(half * 192 + 8 * block)
+
+    def place_24(at, places):
+        for k, place in enumerate(places):
+            sent[place] = turn[pl.ds(pl.multiple_of(at * 8 + 8 * k, 8), 8), :].astype(BF16)
+
+    whiten_half(0)
+
+    @pl.when(core == 0)
+    def _():
+        @pl.loop(0, 8)
+        def _(y0):
+            x_base = [((c + 32 - y0) % 4) * 12 + (y0 // 4) * 3 for c in range(4)]
+            places = []
+            for slot in range(24):
                 z0, r0 = slot // 3, slot % 3
-                x0 = (r0 + 1 - z0 + 32 - y0) % 4
-                place_0 = x0 * 12 + (y0 // 4) * 3 + (z0 * 48 + r0)
-                place_1 = y0 * 48 + ((z0 % 2) * 12 + (z0 // 2) * 3 + r0)
-                put(at, k, jnp.where(on_0, place_0, place_1))
+                places.append(x_base[(r0 + 1 - z0) % 4] + (z0 * 48 + r0))
+            place_24(pl.multiple_of(y0 * 24, 8), places)
+
+    @pl.when(core == 1)
+    def _():
+        @pl.loop(0, 8)
+        def _(y0):
+            places = []
+            for slot in range(24):
+                places.append(y0 * 48 + slot)
+            place_24(pl.multiple_of(y0 * 24, 8), places)
 
     if between is not None:
         between()
 
-    @pl.loop(0, 8)
-    def _(z1):
-        for block in range(3):
-            at = pl.multiple_of(192 + z1 * 24 + 8 * block, 8)
-            whiten_8(at)
-            for k in range(8):
-                x1, slot = (8 * block + k) // 6, (8 * block + k) % 6
+    whiten_half(1)
+
+    @pl.when(core == 0)
+    def _():
+        @pl.loop(0, 8)
+        def _(z1):
+            places = []
+            for n in range(24):
+                x1, slot = n // 6, n % 6
+                places.append(z1 * 48 + (x1 * 12 + 6 + slot))
+            place_24(pl.multiple_of(192 + z1 * 24, 8), places)
+
+    @pl.when(core == 1)
+    def _():
+        @pl.loop(0, 8)
+        def _(z1):
+            y_base = [((c + 32 - z1) % 4) * 48 + z1 * 3 for c in range(4)]
+            places = []
+            for n in range(24):
+                x1, slot = n // 6, n % 6
                 yh1, r1 = slot // 3, slot % 3
-                yl1 = (r1 + 1 - 2 - x1 + 32 - z1) % 4
-                place_0 = z1 * 48 + (x1 * 12 + 6 + slot)
-                place_1 = yl1 * 48 + (z1 % 2) * 12 + (z1 // 2) * 3 + (yh1 * 192 + 24 + r1)
-                put(at, k, jnp.where(on_0, place_0, place_1))
+                places.append(y_base[(r1 + 1 - 2 - x1) % 4] + (yh1 * 192 + 24 + r1))
+            place_24(pl.multiple_of(192 + z1 * 24, 8), places)
 
 
 def gather_blocks(c, got, gram_in):
@@ -180,10 +205,10 @@
 
 
 def make_lhs(z_pair, done_a, done_b, rows_f, lhs_f, lhs_out):
-    for quarter in range(4):
-        of_pair = (z_pair + 4 - quarter) % 4
+    for step in range(4):
+        of_pair = (z_pair + 4 - QUARTERS[step]) % 4
         for y in range(8):
-            values = done_a[y, 6 * quarter : 6 * quarter + 6].astype(F32).reshape(48, 128)
+            values = done_a[y, 6 * step : 6 * step + 6].astype(F32).reshape(48, 128)
             rows_f[pl.ds(pl.multiple_of(of_pair * 48 + y * 192, 16), 48), :] = values
     rows_f[1536:3072] = done_b[...].astype(F32).reshape(1536, 128)
     for b in range(8):
@@ -196,7 +221,7 @@
 
 
 def stack_kernel(
-    wave_hbm, table_hbm, keep_hbm, good_hbm, lhs_out,
+    wave_hbm, table_hbm, keep_hbm, good_hbm, lag_hbm, lhs_out, lag_out,
     wave, table, keep, good,
     spec, mag, turn, sent, mid_a, mid_b, got, gram_in, cross, back_a, back_b, done_a, done_b, rows_f, lhs_f,
     send_sem, recv_sem, local_sem, load_sem,
@@ -262,16 +287,17 @@
             to = next_column(k)
             remote(sent.at[pl.ds(to * 12 + 6 * c, 6)], mid_a.at[column, pl.ds(6 * c, 6)], 0, c, row, to).start()
 
-    def to_rows(c, to_core):
+    def to_rows(to_core):
         @pl.loop(0, 8)
         def _(k):
             to = ((y + ring_8(7 - k)) % 8) * 2 + to_core
 
             @pl.when(to != row)
             def _():
-                remote(sent.at[pl.ds(to * 24 + 12 * c, 12)], mid_b.at[y8, pl.ds(12 * c, 12)], 1, 2 + c, to, column).start()
+                remote(sent.at[pl.ds(to * 24, 24)], mid_b.at[y8], 1, 2, to, column).start()
 
     def first_sends():
+        pltpu.make_async_copy(lag_hbm, lag_out, load_sem.at[6]).start()
         pl.semaphore_wait(barrier, 46)
 
         @pl.when(core == 0)
@@ -280,7 +306,7 @@
 
         @pl.when(core == 1)
         def _():
-            to_rows(0, 0)
+            to_rows(0)
 
     make_units(core, wave, table, keep, good, spec, mag, turn, sent, loaded, first_sends)
 
@@ -291,54 +317,50 @@
 
     @pl.when(core == 1)
     def _():
-        to_rows(0, 1)
-        to_rows(1, 0)
-        to_rows(1, 1)
+        to_rows(1)
         local(sent.at[pl.ds(row * 24, 24)], mid_b.at[y8], 1).start()
 
+    def to_owners_in_column(to_core):
+        @pl.loop(0, 8)
+        def _(k):
+            to = ((y + ring_8(7 - k)) % 8) * 2 + to_core
+
+            @pl.when(jnp.logical_and(share(to, column) != 0, to != row))
+            def _():
+                remote(mid_a.at[:, column_slot(to, column)], got.at[0, y8], 2, 4, to, column).start()
+
+    def to_owners_in_row():
+        @pl.loop(1, 32)
+        def _(k):
+            to = next_column(k)
+
+            @pl.when(share(row, to) != 0)
+            def _():
+                remote(mid_b.at[:, row_slot(row, to)], got.at[1, :, column], 3, 5, row, to).start()
+
     @pl.when(core == 0)
     def _():
         wait_bytes(mid_a.at[0], local_sem.at[0])
+        wait_bytes(mid_a.at[pl.ds(0, 31), pl.ds(0, 6)], recv_sem.at[0])
+        to_owners_in_column(0)
+        wait_bytes(mid_b, recv_sem.at[2])
+        to_owners_in_row()
+        wait_bytes(mid_a.at[pl.ds(0, 31), pl.ds(0, 6)], recv_sem.at[1])
+        to_owners_in_column(1)
 
     @pl.when(core == 1)
     def _():
         wait_bytes(mid_b.at[0], local_sem.at[1])
-
-    for c in range(2):
+        wait_bytes(mid_b.at[pl.ds(0, 7)], recv_sem.at[2])
+        to_owners_in_row()
+
+    @pl.when(owner)
+    def _():
         @pl.when(core == 0)
         def _():
-            wait_bytes(mid_a.at[pl.ds(0, 31), pl.ds(0, 6)], recv_sem.at[c])
-
-            @pl.loop(0, 8)
-            def _(k):
-                to = ((y + ring_8(7 - k)) % 8) * 2 + c
-
-                @pl.when(jnp.logical_and(share(to, column) != 0, to != row))
-                def _():
-                    remote(mid_a.at[:, column_slot(to, column)], got.at[0, y8], 2, 4, to, column).start()
-
-            wait_bytes(mid_b.at[:, pl.ds(0, 12)], recv_sem.at[2 + c])
-
-        @pl.when(core == 1)
-        def _():
-            wait_bytes(mid_b.at[pl.ds(0, 7), pl.ds(0, 12)], recv_sem.at[2 + c])
-
-        @pl.loop(0, 16)
-        def _(k):
-            back = 15 - k
-            to = ((z + (z + c) % 2 + 2 * ring_4(back % 4)) % 8) * 4 + (x + ring_4(back // 4)) % 4
-
-            @pl.when(jnp.logical_and(share(row, to) != 0, to != column))
-            def _():
-                remote(mid_b.at[:, row_slot_by_parity(row, to)], got.at[1, :, column], 3, 5, row, to).start()
-
-    @pl.when(owner)
-    def _():
-        @pl.when(core == 0)
-        def _():
             local(mid_a.at[:, column_slot(row, column)], got.at[0, y8], 2).start()
 
-        local(mid_b.at[:, row_slot_by_parity(row, column)], got.at[1, :, column], 3).start()
+        local(mid_b.at[:, row_slot(row, column)], got.at[1, :, column], 3).start()
         @pl.when(core == 0)
         def _():
             wait_bytes(got.at[0, 0], local_sem.at[2])
@@ -357,9 +379,9 @@
         slot_b = column_slot(row, column) % 6
 
         @pl.loop(0, 4)
-        def _(quarter):
-            pair = (quarter + z // 2) % 4
-            to_hi, half = (quarter // 2 + 1 - y // 4) % 2, quarter % 2
+        def _(step):
+            pair = (quarter_of(step) + z // 2) % 4
+            to_hi, half = (step // 2 + 1 - y // 4) % 2, step % 2
             first = jnp.where(core == 0, pair, to_hi * 4 + half)
             second = jnp.where(core == 0, pair + 4, to_hi * 4 + half + 2)
             cross_of(core, (first, second), gram_in, cross)
@@ -369,11 +391,11 @@
                 @pl.loop(0, 8)
                 def _(k):
                     to = pair * 8 + (column + k + 1) % 8
-                    slot = quarter * 6 + slot_a
+                    slot = step * 6 + slot_a
 
                     @pl.when(to != column)
                     def _():
-                        remote(cross.at[pl.ds(to * 16, 16)], back_a.at[slot], 4, 6 + quarter // 2, row, to).start()
+                        remote(cross.at[pl.ds(to * 16, 16)], back_a.at[slot], 4, 6 + step // 2, row, to).start()
 
                     @pl.when(to == column)
                     def _():
@@ -402,20 +424,20 @@
     def _():
         wait_bytes(back_b.at[0], local_sem.at[5])
 
-    for c in range(2):
-        @pl.when(core == 0)
-        def _():
-            if c == 0:
+    @pl.when(core == 0)
+    def _():
+        for c in range(2):
+            if c == 1:
                 @pl.when(own_a)
                 def _():
                     wait_bytes(back_a.at[0], local_sem.at[4])
-                    wait_bytes(back_a.at[pl.ds(0, 11)], recv_sem.at[6])
+                    wait_bytes(back_a.at[pl.ds(0, 11)], recv_sem.at[7])
 
                 @pl.when(jnp.logical_not(own_a))
                 def _():
-                    wait_bytes(back_a.at[pl.ds(0, 12)], recv_sem.at[6])
+                    wait_bytes(back_a.at[pl.ds(0, 12)], recv_sem.at[7])
             else:
-                wait_bytes(back_a.at[pl.ds(0, 12)], recv_sem.at[7])
+                wait_bytes(back_a.at[pl.ds(0, 12)], recv_sem.at[6])
 
             @pl.loop(1, 16)
             def _(k):
@@ -423,6 +445,7 @@
                 slots = pl.ds(12 * c, 12)
                 remote(back_a.at[slots, to], done_a.at[y, slots], 6, 10, to, column).start()
 
+    for c in range(2):
         @pl.when(own_b)
         def _():
             wait_bytes(back_b.at[pl.ds(0, 5), pl.ds(0, 16)], recv_sem.at[8 + c])
@@ -459,6 +482,8 @@
     wait_bytes(done_b.at[pl.ds(0, 31)], recv_sem.at[11])
     make_lhs(z // 2, done_a, done_b, rows_f, lhs_f, lhs_out)
 
+    pltpu.make_async_copy(lag_hbm, lag_out, load_sem.at[6]).wait()
+
     @pl.when(core == 0)
     def _():
         wait_bytes(mid_a.at[pl.ds(0, 31)], send_sem.at[0])
@@ -496,13 +521,13 @@
     wait_bytes(done_b.at[pl.ds(0, 31)], send_sem.at[7])
 
 
-def stacked(wave, table, keep, good):
+def stacked(wave, table, keep, good, lag):
     in_hbm = pl.BlockSpec(memory_space=pltpu.HBM)
     return pl.pallas_call(
         stack_kernel,
-        out_shape=jax.ShapeDtypeStruct((512, 2 * BINS), BF16),
-        in_specs=[in_hbm] * 4,
-        out_specs=pl.BlockSpec(memory_space=pltpu.VMEM),
+        out_shape=(pltpu.VMEM((512, 2 * BINS), BF16), pltpu.VMEM((2 * BINS, LAGS), BF16)),
+        in_specs=[in_hbm] * 5,
+        out_specs=(pl.BlockSpec(memory_space=pltpu.VMEM),) * 2,
         scratch_shapes=[
             pltpu.VMEM((512, NT), BF16),
             pltpu.VMEM((2 * BINS, NT), BF16),
@@ -526,11 +551,11 @@
             pltpu.SemaphoreType.DMA((8,)),
             pltpu.SemaphoreType.DMA((12,)),
             pltpu.SemaphoreType.DMA((8,)),
-            pltpu.SemaphoreType.DMA((6,)),
+            pltpu.SemaphoreType.DMA((7,)),
         ],
         compiler_params=pltpu.CompilerParams(collective_id=0, has_side_effects=True, vmem_limit_bytes=48 << 20),
         name="stack_cross_spectra",
-    )(*[pltpu.with_memory_space_constraint(value, pltpu.HBM) for value in (wave, table, keep, good)])
+    )(*[pltpu.with_memory_space_constraint(value, pltpu.HBM) for value in (wave, table, keep, good, lag)])
 
 
 def lag_kernel(scale, lhs, table, out, block, sem):
@@ -561,8 +586,10 @@
 
 def local(waveforms, segment_keep, channel_good):
     wave = waveforms.reshape(512, NT)
-    lhs = stacked(wave, jnp.asarray(forward_rows()), segment_keep, channel_good.reshape(1, 64))
-    return lagged(lhs, jnp.asarray(lag_rows()), float(1.0 / np.sqrt(SEGS * BINS)))
+    lhs, lag = stacked(
+        wave, jnp.asarray(forward_rows()), segment_keep, channel_good.reshape(1, 64), jnp.asarray(lag_rows())
+    )
+    return lagged(lhs, lag, float(1.0 / np.sqrt(SEGS * BINS)))
 
 
 def solution(mesh):

time: 70.3 us -> 66.7 us (0.949)
  the two profiles are of different devices: /device:TPU:1 before, /device:TPU:64 now
where the time goes in v3:
time: 66.7 us; the launch traced here: 66.6 us
  Pallas kernels  66.6 us (100%)
    pallas_call x1, Pallas kernels, stacked(): pl.pallas_call(stack_kernel, out_shape=(pltpu.VMEM((512, 2 * BINS), BF16)...  63.3 us
    pallas_call x1, Pallas kernels, lagged(): pl.pallas_call(functools.partial(lag_kernel, scale), out_shape=jax.ShapeD...  3.28 us

profile of v3, /device:TPU:64, one launch (start us, length us, event | category | flops | bytes accessed | tf_op | source)
XLA Modules:
  0.0 66.6 jit_solution(12701500815500167504)
XLA Ops:
  0.0 63.3 %stack_cross_spectra.1 = (bf16[512,768]{1,0:T(8,128)(2,1)S(1)}, bf16[768,2560]{1,0:T(8,128)(2,1)S(1)}) custom-call(bf16[512,1536]{1,0:T(8,128)(2,1)} %bitcast.2, bf16[768,1536]{1,0:T(8,128)(2,1)} %constant.4.clone.table_hbm, s32[8]{0:T(128)} %keep_hbm.1, s32[1,64]{1,0:T(1,128)} %bitcast.3, bf16[768,2560]{1,0:T(8,128)(2,1)} %constant.5.clone.lag_hbm), custom_call_target="tpu_custom_call" | custom-call | tf_op jit(solution)/shard_map/stack_cross_spectra/pallas_call | solution.py:526
  63.3 3.3 %lag_transform.1 = bf16[64,8,2560]{2,1,0:T(8,128)(2,1)} custom-call(bf16[512,768]{1,0:T(8,128)(2,1)S(1)} %get-tuple-element.7.lhs, bf16[768,2560]{1,0:T(8,128)(2,1)S(1)} %get-tuple-element.8.table), custom_call_target="tpu_custom_call" | custom-call | tf_op jit(solution)/shard_map/lag_transform/pallas_call | solution.py:576

commit v4 on v3

--- a/solution.py
+++ b/solution.py
@@ -259,11 +259,11 @@
 
     @pl.loop(1, 32)
     def _(k):
-        pl.semaphore_signal(barrier, inc=1, device_id=device_of(row, next_column(k)), device_id_type=MESH)
+        pl.semaphore_signal(barrier, inc=1, device_id=(chan, seg - column + (column + k) % 32), device_id_type=MESH)
 
     @pl.loop(1, 16)
     def _(k):
-        pl.semaphore_signal(barrier, inc=1, device_id=device_of(next_row(k), column), device_id_type=MESH)
+        pl.semaphore_signal(barrier, inc=1, device_id=device_of((row + k) % 16, column), device_id_type=MESH)
 
     def remote(src, dst, n, m, to_row, to_column):
         return pltpu.make_async_remote_copy(
@@ -297,7 +297,6 @@
                 remote(sent.at[pl.ds(to * 24, 24)], mid_b.at[y8], 1, 2, to, column).start()
 
     def first_sends():
-        pltpu.make_async_copy(lag_hbm, lag_out, load_sem.at[6]).start()
         pl.semaphore_wait(barrier, 46)
 
         @pl.when(core == 0)
@@ -319,6 +318,8 @@
     def _():
         to_rows(1)
         local(sent.at[pl.ds(row * 24, 24)], mid_b.at[y8], 1).start()
+
+    pltpu.make_async_copy(lag_hbm, lag_out, load_sem.at[6]).start()
 
     def to_owners_in_column(to_core):
         @pl.loop(0, 8)
@@ -342,9 +343,9 @@
     def _():
         wait_bytes(mid_a.at[0], local_sem.at[0])
         wait_bytes(mid_a.at[pl.ds(0, 31), pl.ds(0, 6)], recv_sem.at[0])
-        to_owners_in_column(0)
         wait_bytes(mid_b, recv_sem.at[2])
         to_owners_in_row()
+        to_owners_in_column(0)
         wait_bytes(mid_a.at[pl.ds(0, 31), pl.ds(0, 6)], recv_sem.at[1])
         to_owners_in_column(1)
 
@@ -559,16 +560,17 @@
 
 
 def lag_kernel(scale, lhs, table, out, block, sem):
-    width = block.shape[-1]
-    count = LAGS // width
-    for n in range(count):
-        if n >= 2:
-            pltpu.make_async_copy(block.at[n % 2], out.at[:, :, pl.ds((n - 2) * width, width)], sem.at[n % 2]).wait()
-        values = jnp.dot(lhs[...], table[:, n * width : (n + 1) * width], preferred_element_type=F32) * scale
-        block[n % 2] = values.reshape(64, 8, width).astype(BF16)
-        pltpu.make_async_copy(block.at[n % 2], out.at[:, :, pl.ds(n * width, width)], sem.at[n % 2]).start()
-    for n in range(count - 2, count):
-        pltpu.make_async_copy(block.at[n % 2], out.at[:, :, pl.ds(n * width, width)], sem.at[n % 2]).wait()
+    width = 512
+    copies = []
+    for n in range(LAGS // width):
+        cols = slice(n * width, (n + 1) * width)
+        values = jnp.dot(lhs[...], table[:, cols], preferred_element_type=F32) * scale
+        block[:, :, cols] = values.reshape(64, 8, width).astype(BF16)
+        at = pl.ds(n * width, width)
+        copies.append(pltpu.make_async_copy(block.at[:, :, at], out.at[:, :, at], sem.at[n]))
+        copies[-1].start()
+    for copy in copies:
+        copy.wait()
 
 
 def lagged(lhs, table, scale):
@@ -578,8 +580,8 @@
         out_shape=jax.ShapeDtypeStruct((64, 8, LAGS), BF16),
         in_specs=[vmem, vmem],
         out_specs=pl.BlockSpec(memory_space=pl.ANY),
-        scratch_shapes=[pltpu.VMEM((2, 64, 8, LAGS // 2), BF16), pltpu.SemaphoreType.DMA((2,))],
-        compiler_params=pltpu.CompilerParams(vmem_limit_bytes=48 << 20),
+        scratch_shapes=[pltpu.VMEM((64, 8, LAGS), BF16), pltpu.SemaphoreType.DMA((5,))],
+        compiler_params=pltpu.CompilerParams(vmem_limit_bytes=32 << 20),
         name="lag_transform",
     )(lhs, table)
 

time: 66.7 us -> 65 us (0.975)
  the two profiles are of different devices: /device:TPU:64 before, /device:TPU:1 now
where the time goes in v4:
time: 65 us; the launch traced here: 64.2 us
  Pallas kernels  64.2 us (99%)
    pallas_call x1, Pallas kernels, stacked(): pl.pallas_call(stack_kernel, out_shape=(pltpu.VMEM((512, 2 * BINS), BF16)...  61.2 us
    pallas_call x1, Pallas kernels, lagged(): pl.pallas_call(functools.partial(lag_kernel, scale), out_shape=jax.ShapeD...  3.04 us

profile of v4, /device:TPU:1, one launch (start us, length us, event | category | flops | bytes accessed | tf_op | source)
XLA Modules:
  0.0 64.2 jit_solution(14593294413712019954)
XLA Ops:
  0.0 61.2 %stack_cross_spectra.1 = (bf16[512,768]{1,0:T(8,128)(2,1)S(1)}, bf16[768,2560]{1,0:T(8,128)(2,1)S(1)}) custom-call(bf16[512,1536]{1,0:T(8,128)(2,1)} %bitcast.2, bf16[768,1536]{1,0:T(8,128)(2,1)} %constant.4.clone.table_hbm, s32[8]{0:T(128)} %keep_hbm.1, s32[1,64]{1,0:T(1,128)} %bitcast.3, bf16[768,2560]{1,0:T(8,128)(2,1)} %constant.5.clone.lag_hbm), custom_call_target="tpu_custom_call" | custom-call | tf_op jit(solution)/shard_map/stack_cross_spectra/pallas_call | solution.py:527
  61.2 3.0 %lag_transform.1 = bf16[64,8,2560]{2,1,0:T(8,128)(2,1)} custom-call(bf16[512,768]{1,0:T(8,128)(2,1)S(1)} %get-tuple-element.7.lhs, bf16[768,2560]{1,0:T(8,128)(2,1)S(1)} %get-tuple-element.8.table), custom_call_target="tpu_custom_call" | custom-call | tf_op jit(solution)/shard_map/lag_transform/pallas_call | solution.py:578

commit v5 on v4

--- a/solution.py
+++ b/solution.py
@@ -257,12 +257,9 @@
 
     barrier = pltpu.get_barrier_semaphore()
 
-    @pl.loop(1, 32)
-    def _(k):
+    for k in range(1, 32):
         pl.semaphore_signal(barrier, inc=1, device_id=(chan, seg - column + (column + k) % 32), device_id_type=MESH)
-
-    @pl.loop(1, 16)
-    def _(k):
+    for k in range(1, 16):
         pl.semaphore_signal(barrier, inc=1, device_id=device_of((row + k) % 16, column), device_id_type=MESH)
 
     def remote(src, dst, n, m, to_row, to_column):

time: 65 us -> 65.3 us (level)
  the two profiles are of different devices: /device:TPU:1 before, /device:TPU:6 now
where the time goes in v5:
time: 65.3 us; the launch traced here: 65.2 us
  Pallas kernels  65.2 us (100%)
    pallas_call x1, Pallas kernels, stacked(): pl.pallas_call(stack_kernel, out_shape=(pltpu.VMEM((512, 2 * BINS), BF16)...  62.2 us
    pallas_call x1, Pallas kernels, lagged(): pl.pallas_call(functools.partial(lag_kernel, scale), out_shape=jax.ShapeD...  3.04 us

profile of v5, /device:TPU:6, one launch (start us, length us, event | category | flops | bytes accessed | tf_op | source)
XLA Modules:
  0.0 65.2 jit_solution(13893780688971551571)
XLA Ops:
  0.0 62.2 %stack_cross_spectra.1 = (bf16[512,768]{1,0:T(8,128)(2,1)S(1)}, bf16[768,2560]{1,0:T(8,128)(2,1)S(1)}) custom-call(bf16[512,1536]{1,0:T(8,128)(2,1)} %bitcast.2, bf16[768,1536]{1,0:T(8,128)(2,1)} %constant.4.clone.table_hbm, s32[8]{0:T(128)} %keep_hbm.1, s32[1,64]{1,0:T(1,128)} %bitcast.3, bf16[768,2560]{1,0:T(8,128)(2,1)} %constant.5.clone.lag_hbm), custom_call_target="tpu_custom_call" | custom-call | tf_op jit(solution)/shard_map/stack_cross_spectra/pallas_call | solution.py:524
  62.2 3.0 %lag_transform.1 = bf16[64,8,2560]{2,1,0:T(8,128)(2,1)} custom-call(bf16[512,768]{1,0:T(8,128)(2,1)S(1)} %get-tuple-element.7.lhs, bf16[768,2560]{1,0:T(8,128)(2,1)S(1)} %get-tuple-element.8.table), custom_call_target="tpu_custom_call" | custom-call | tf_op jit(solution)/shard_map/lag_transform/pallas_call | solution.py:575
